TPU v7x, 32 devices: a whole 2x2x4 slice. The times are simulated.
32 devices in a mesh: seq: 16 (over z, y, core), kv: 2 (over x).
Axes of the slice: x: 2, y: 2, z: 4, core: 2. Of those that a mesh axis runs over, the one named last changes fastest.
Arguments:
- plan: int32 [16], replicated, may hold values from 0 to 15, each once
- queries: bfloat16 [2048, 1024], P('seq', 'kv'), may hold values from -24 to 24
- keys: bfloat16 [2048, 256], P('seq', 'kv'), may hold values from -9 to 9
- student_c: bfloat16 [2048, 1024], P('seq', 'kv'), may hold values from -0.125 to 0.125
- layer_input: bfloat16 [2048, 8192], P('seq', 'kv'), may hold values from -6 to 6
- b_weight: bfloat16 [2, 8192, 128], P('kv'), may hold values from -0.0625 to 0.0625
Outputs:
- grad_c: bfloat16 [2048, 1024], P('seq', 'kv')
- grad_wb: float32 [2, 8192, 128], P('kv', 'seq')
Inputs may be any that keep to these rules, and one draw needn't show every extreme that they name: Each value appears once: plan[d] is the block of 128 consecutive positions held by index d of seq.
All inputs are finite; a program needn't handle non-finite values.
Results may differ from a plain program's by a relative error of at most 0.0049.
Values may be sent and summed in bfloat16 or wider, within the bound.
A program may use at most 64 MiB of HBM per device.

v0:
```python
import math

import jax
import jax.numpy as jnp
from jax import lax
from jax.sharding import PartitionSpec as P

NEG_FILL = -1e30


def block_sweep(update, running, pieces, shard_rows):
    total_rows = pieces[0].shape[0]
    shard_count = total_rows // shard_rows
    block_limit = max(1, 1024 // shard_rows)
    factor = 1
    for option in range(1, shard_count + 1):
        if shard_count % option == 0 and option <= block_limit:
            factor = option
    block_rows = factor * shard_rows
    block_count = total_rows // block_rows
    stacked = tuple(
        (member.reshape((block_count, block_rows) + member.shape[1:]) for member in pieces)
    )
    offsets = block_rows * jnp.arange(block_count, dtype=jnp.int32)

    def advance(partial_state, inputs):
        return (update(partial_state, inputs[0], inputs[1]), None)

    running, unused = lax.scan(advance, running, (stacked, offsets))
    return running


def local(plan, queries, keys, student_c, layer_input, b_weight):
    shard_rows = keys.shape[0]
    state_width = keys.shape[1]
    head_count = queries.shape[1] // state_width
    seq_count = lax.axis_size("seq")
    token_count = shard_rows * seq_count
    student_scale = 2.0 / math.sqrt(token_count)
    score_scale = 1.0 / math.sqrt(state_width)
    block_ids = jnp.arange(seq_count, dtype=jnp.int32)

    def positions_of(global_rows):
        owner_ids = global_rows // shard_rows
        picked = jnp.sum(
            jnp.where(owner_ids[:, None] == block_ids[None, :], plan[None, :], 0), axis=1
        )
        return picked * shard_rows + global_rows % shard_rows

    own_start = lax.axis_index("seq") * shard_rows
    query_pos = positions_of(own_start + jnp.arange(shard_rows, dtype=jnp.int32))
    query_heads = queries.reshape(shard_rows, head_count, state_width)
    student_heads = student_c.reshape(shard_rows, head_count, state_width)
    features = lax.all_gather(layer_input, "kv", axis=1, tiled=True)
    b_local = jnp.dot(features, b_weight[0], preferred_element_type=jnp.float32).astype(
        jnp.bfloat16
    )

    def scores_of(key_block, offset):
        key_pos = positions_of(offset + jnp.arange(key_block.shape[0], dtype=jnp.int32))
        visible = key_pos[None, None, :] <= query_pos[:, None, None]
        scores = (
            jnp.einsum("qhd,kd->qhk", query_heads, key_block, preferred_element_type=jnp.float32)
            * score_scale
        )
        return (jnp.where(visible, scores, NEG_FILL), visible)

    def stats_step(running, members, offset):
        highest, totals = running
        scores, visible = scores_of(members[0], offset)
        raised = jnp.maximum(highest, jnp.max(scores, axis=-1))
        weights = jnp.where(visible, jnp.exp(scores - raised[..., None]), 0.0)
        return (raised, totals * jnp.exp(highest - raised) + jnp.sum(weights, axis=-1))

    def pair_step(highest, totals):

        def advance_pair(running, members, offset):
            grad_acc, db_buffer = running
            key_block, b_block = members
            scores, visible = scores_of(key_block, offset)
            teacher = jnp.where(
                visible, jnp.exp(scores - highest[..., None]) / totals[..., None], 0.0
            )
            student = student_scale * jnp.einsum(
                "qhd,kd->qhk", student_heads, b_block, preferred_element_type=jnp.float32
            )
            residual = jnp.where(visible, student - teacher, 0.0).astype(jnp.bfloat16)
            grad_acc = grad_acc + jnp.einsum(
                "qhk,kd->qhd", residual, b_block, preferred_element_type=jnp.float32
            )
            contrib = jnp.einsum(
                "qhk,qhd->kd", residual, student_heads, preferred_element_type=jnp.float32
            )
            db_buffer = lax.dynamic_update_slice_in_dim(db_buffer, contrib, offset, 0)
            return (grad_acc, db_buffer)

        return advance_pair

    stats_init = (
        jnp.full((shard_rows, head_count), NEG_FILL, jnp.float32),
        jnp.zeros((shard_rows, head_count), jnp.float32),
    )
    pair_init = (
        jnp.zeros((shard_rows, head_count, state_width), jnp.float32),
        jnp.zeros((token_count, state_width), jnp.float32),
    )
    highest, totals = block_sweep(
        stats_step, stats_init, (lax.all_gather(keys, "seq", axis=0, tiled=True),), shard_rows
    )
    advance_pair = pair_step(highest, totals)
    grad_acc, db_buffer = block_sweep(
        advance_pair,
        pair_init,
        (
            lax.all_gather(keys, "seq", axis=0, tiled=True),
            lax.all_gather(b_local, "seq", axis=0, tiled=True),
        ),
        shard_rows,
    )
    arrived = lax.all_to_all(
        db_buffer.reshape(seq_count, shard_rows, state_width).astype(jnp.bfloat16),
        "seq",
        split_axis=0,
        concat_axis=0,
        tiled=True,
    ).astype(jnp.float32)
    b_grad = jnp.sum(arrived, axis=0).astype(jnp.bfloat16)
    weight_grad = lax.psum_scatter(
        jnp.einsum("td,tn->dn", features, b_grad, preferred_element_type=jnp.float32),
        "seq",
        scatter_dimension=0,
        tiled=True,
    )
    grad_c = grad_acc.reshape(shard_rows, head_count * state_width).astype(jnp.bfloat16)
    return (grad_c, weight_grad[None])


def solution(mesh):
    in_specs = (
        P(),
        P("seq", "kv"),
        P("seq", "kv"),
        P("seq", "kv"),
        P("seq", "kv"),
        P("kv", None, None),
    )
    out_specs = (P("seq", "kv"), P("kv", "seq", None))
    return jax.shard_map(local, mesh=mesh, in_specs=in_specs, out_specs=out_specs, check_vma=False)
```

profile of v0, /device:TPU:0, one launch (start us, length us, event | category | flops | bytes accessed | tf_op | source)
XLA Modules:
  0.0 205.9 jit_solution(17083190945803974519)
XLA Ops:
  7.2 0.0 copy-start
  7.2 0.0 copy-start.3
  7.2 0.0 copy-start.2
  7.2 0.0 all-gather.2.cloned.1.call-start
  7.2 0.7 all-gather.2.cloned.1.call-update
  7.9 0.0 reduce-scatter.2.cloned.1.call-start
  8.0 0.5 iota_multiply_fusion
  8.5 0.7 select_reduce_fusion.3
  9.3 26.4 %all_gather.12 = bf16[2048,128]{1,0:T(8,128)(2,1)} all-gather(bf16[128,128]{1,0:T(8,128)(2,1)} %param.12), channel_id=1, replica_groups=mesh['seq'=16,'kv'=2] {'seq'}, dimensions={0}, use_global_device_ids=true | all-gather | bytes 557056 | tf_op jit(solution)/shard_map/all_gather | solution.py:115
  35.6 1.0 copy.21
  36.7 0.8 copy.24
  37.5 0.0 copy-done.2
  37.5 0.1 copy.20
  37.6 0.1 copy.23
  37.7 0.0 copy-done.3
  37.7 15.4 %while.30 = (s32[]{:T(128)}, f32[128,4]{0,1:T(4,128)S(1)}, f32[128,4]{0,1:T(4,128)S(1)}, s32[2]{0:T(128)}, s32[16]{0:T(128)S(1)}, /*index=5*/s32[128]{0:T(128)S(...) while((s32[]{:T(128)}, f32[128,4]{0,1:T(4,128)S(1)}, ...), condition=%wide.region_5.6_spmd.clone, body=%wide.region_1.5_spmd.clone.sunk | while | flops 138624512 | bytes 5033156 | solution.py:29
  37.7 1.2 dynamic_slice.62
  38.9 0.6 add_select_fusion.6
  39.6 0.1 select_reduce_fusion.7
  39.7 0.6 fusion.70
  40.3 0.2 broadcast_compare_fusion.4
  40.5 2.8 %fusion.71 = (f32[128,4]{0,1:T(4,128)S(1)}, f32[1024,128,4]{1,0,2:T(8,128)}) fusion(pred[128,1024]{0,1:T(8,128)(4,1)S(1)} %broadcast_compare_fusion.4, bf16[128,4,128]{2,0,1:T(8,128)(2,1)} %get-tuple-element.599, bf16[2,1024,128]{2,1,0:T(8,128)(2,1)} %get-tuple-element.598, s32[]{:T(128)} %get-tuple-element.582), kind=kOutput, calls=%fused_computation.4.clone.1 | convolution fusion | flops 135790080 | bytes 2624000 | tf_op jit(solution)/shard_map/while/body/eval_jaxpr/qhd,kd->qhk/dot_general | solution.py:63
  43.3 2.1 %select_reduce_fusion.8 = f32[128,4]{0,1:T(4,128)S(1)} fusion(f32[1024,128,4]{1,0,2:T(8,128)} %get-tuple-element.559, f32[128,4]{0,1:T(4,128)S(1)} %select_maximum_fusion.2, pred[128,1024]{0,1:T(8,128)(4,1)S(1)} %broadcast_compare_fusion.4), kind=kLoop, calls=%fused_computation.3.clone.1 | loop fusion | flops 2620928 | bytes 2232320 | tf_op jit(solution)/shard_map/while/body/eval_jaxpr/reduce_sum | solution.py:73
  45.4 1.2 dynamic_slice.62
  46.6 0.6 add_select_fusion.6
  47.3 0.1 select_reduce_fusion.7
  47.3 0.6 fusion.70
  48.0 0.2 broadcast_compare_fusion.4
  48.2 2.8 %fusion.71 = (f32[128,4]{0,1:T(4,128)S(1)}, f32[1024,128,4]{1,0,2:T(8,128)}) fusion(pred[128,1024]{0,1:T(8,128)(4,1)S(1)} %broadcast_compare_fusion.4, bf16[128,4,128]{2,0,1:T(8,128)(2,1)} %get-tuple-element.599, bf16[2,1024,128]{2,1,0:T(8,128)(2,1)} %get-tuple-element.598, s32[]{:T(128)} %get-tuple-element.582), kind=kOutput, calls=%fused_computation.4.clone.1 | convolution fusion | flops 135790080 | bytes 2624000 | tf_op jit(solution)/shard_map/while/body/eval_jaxpr/qhd,kd->qhk/dot_general | solution.py:63
  51.0 2.1 %select_reduce_fusion.8 = f32[128,4]{0,1:T(4,128)S(1)} fusion(f32[1024,128,4]{1,0,2:T(8,128)} %get-tuple-element.559, f32[128,4]{0,1:T(4,128)S(1)} %select_maximum_fusion.2, pred[128,1024]{0,1:T(8,128)(4,1)S(1)} %broadcast_compare_fusion.4), kind=kLoop, calls=%fused_computation.3.clone.1 | loop fusion | flops 2620928 | bytes 2232320 | tf_op jit(solution)/shard_map/while/body/eval_jaxpr/reduce_sum | solution.py:73
  53.1 0.0 all-gather.2.cloned.1.call-done
  53.2 0.0 copy-done
  53.2 2.3 %fusion.41 = bf16[128,128]{1,0:T(8,128)(2,1)S(1)} fusion(bf16[128,8192]{1,0:T(8,128)(2,1)} %all-gather.2.cloned.1.call-done, bf16[1,8192,128]{2,1,0:T(8,128)(2,1)S(1)} %copy-done), kind=kOutput, calls=%fused_computation.67 | convolution fusion | flops 268451840 | bytes 4227072 | tf_op jit(solution)/shard_map/dot_general | solution.py:55
  55.5 20.3 %all_gather.11 = bf16[2048,128]{1,0:T(8,128)(2,1)} all-gather(bf16[128,128]{1,0:T(8,128)(2,1)S(1)} %fusion.41), channel_id=1, replica_groups=mesh['seq'=16,'kv'=2] {'seq'}, dimensions={0}, use_global_device_ids=true | all-gather | bytes 557056 | tf_op jit(solution)/shard_map/all_gather | solution.py:116
  75.7 0.9 broadcast_in_dim.132
  76.6 26.1 %while.31 = (s32[]{:T(128)}, f32[128,4,128]{2,0,1:T(8,128)}, bf16[2048,128]{1,0:T(8,128)(2,1)}, s32[2]{0:T(128)}, s32[16]{0:T(128)S(1)}, /*index=5*/s32[128]{0:T...) while((s32[]{:T(128)}, f32[128,4,128]{2,0,1:T(8,128)}, ...), condition=%wide.region_8.9_spmd.clone, body=%wide.region_6.8_spmd.clone.sunk | while | flops 541930496 | bytes 10123537 | solution.py:29
  76.6 1.3 dynamic_slice.66
  77.8 0.6 add_select_fusion.7
  78.5 0.1 select_reduce_fusion.9
  78.6 0.6 fusion.82
  79.2 0.2 broadcast_compare_fusion.5
  79.4 1.4 fusion.81
  80.8 2.0 fusion.83
  82.8 0.4 convolution_bitcast_fusion.3
  85.2 2.7 %dynamic_update_slice.8 = bf16[2048,128]{1,0:T(8,128)(2,1)} dynamic-update-slice(bf16[2048,128]{1,0:T(8,128)(2,1)} %get-tuple-element.619, bf16[1024,128]{1,0:T(8,128)(2,1)S(1)} %convolution_bitcast_fusion.3, s32[]{:T(128)S(6)} %select_n.206, s32[]{:T(128)} %constant.191.clone.1..sunk.1) | dynamic-update-slice | bytes 524292 | tf_op jit(solution)/shard_map/while/body/eval_jaxpr/dynamic_update_slice | solution.py:94
  87.9 2.1 %convolution_add_fusion.2 = f32[128,4,128]{2,0,1:T(8,128)} fusion(bf16[128,4,1024]{0,2,1:T(8,128)(2,1)S(1)} %fusion.83, f32[128,4,128]{2,0,1:T(8,128)} %get-tuple-element.618, bf16[2,1024,128]{2,1,0:T(8,128)(2,1)} %get-tuple-element.638, s32[]{:T(128)} %get-tuple-element.617, pred[]{:T(512)S(6)} %compare.39), kind=kOutput, calls=%fused_computation.37.clone.1 | convolution fusion | flops 134348800 | bytes 1835521 | tf_op jit(solution)/shard_map/while/body/eval_jaxpr/qhk,kd->qhd/dot_general | solution.py:88
  90.1 1.3 dynamic_slice.66
  91.3 0.6 add_select_fusion.7
  92.0 0.1 select_reduce_fusion.9
  92.1 0.6 fusion.82
  92.7 0.2 broadcast_compare_fusion.5
  92.9 1.4 fusion.81
  94.3 2.0 fusion.83
  96.3 0.4 convolution_bitcast_fusion.3
  98.7 1.8 dynamic_update_slice.8
  100.5 2.2 %convolution_add_fusion.2 = f32[128,4,128]{2,0,1:T(8,128)} fusion(bf16[128,4,1024]{0,2,1:T(8,128)(2,1)S(1)} %fusion.83, f32[128,4,128]{2,0,1:T(8,128)} %get-tuple-element.618, bf16[2,1024,128]{2,1,0:T(8,128)(2,1)} %get-tuple-element.638, s32[]{:T(128)} %get-tuple-element.617, pred[]{:T(512)S(6)} %compare.39), kind=kOutput, calls=%fused_computation.37.clone.1 | convolution fusion | flops 134348800 | bytes 1835521 | tf_op jit(solution)/shard_map/while/body/eval_jaxpr/qhk,kd->qhd/dot_general | solution.py:88
  102.7 18.0 %all_to_all.5 = bf16[16,128,128]{2,1,0:T(8,128)(2,1)S(1)} all-to-all(bf16[16,128,128]{2,1,0:T(8,128)(2,1)} %bitcast.107), channel_id=1, replica_groups=mesh['seq'=16,'kv'=2] {'seq'}, dimensions={0} | all-to-all | bytes 1048576 | tf_op jit(solution)/shard_map/all_to_all | solution.py:120
  120.7 0.1 reduce_sum.58
  120.8 4.2 %convolution_bitcast_fusion.1 = f32[8192,128]{0,1:T(8,128)} fusion(bf16[128,128]{1,0:T(8,128)(2,1)S(1)} %reduce_sum.58, bf16[128,8192]{1,0:T(8,128)(2,1)} %all-gather.2.cloned.1.call-done), kind=kOutput, calls=%fused_computation.64 | convolution fusion | flops 268435456 | bytes 6324224 | tf_op jit(solution)/shard_map/td,tn->dn/dot_general | solution.py:129
  125.0 0.0 reduce-scatter.2.cloned.1.call-update
  125.0 0.9 copy-done.1
  126.0 0.7 copy_bitcast_fusion
  126.6 70.7 %reduce-scatter.2.cloned.1.call-done = f32[512,128]{0,1:T(8,128)} async-done(((f32[8192,128]{0,1:T(8,128)}), f32[512,128]{0,1:T(8,128)}) %reduce-scatter.2.cloned.1.call-update) | async-done | bytes 262160 | tf_op jit(solution)/shard_map/reduce_scatter | solution.py:128
  197.3 1.8 copy.26
  (12 shorter events, 0.1 us)
Async XLA Ops:
  7.2 46.0 %copy-start = (bf16[1,8192,128]{2,1,0:T(8,128)(2,1)S(1)}, bf16[1,8192,128]{2,1,0:T(8,128)(2,1)}, u32[]{:S(2)}) copy-start(bf16[1,8192,128]{2,1,0:T(8,128)(2,1)} %param.15) | copy-start | bytes 6291460
  7.2 30.5 %copy-start.3 = (s32[16]{0:T(128)S(1)}, s32[16]{0:T(128)}, u32[]{:S(2)}) copy-start(s32[16]{0:T(128)} %param.10) | copy-start | bytes 196
  7.2 30.3 %copy-start.2 = (bf16[128,512]{1,0:T(8,128)(2,1)S(1)}, bf16[128,512]{1,0:T(8,128)(2,1)}, u32[]{:S(2)}) copy-start(bf16[128,512]{1,0:T(8,128)(2,1)} %param.13) | copy-start | bytes 393220
  7.2 45.9 %all-gather.2.cloned.1.call-start = ((), (), s32[]{:S(2)}) async-start(), calls=%async_computation.2 | async-start | bytes 3145728 | tf_op jit(solution)/shard_map/all_gather | solution.py:54
  7.9 189.4 %reduce-scatter.2.cloned.1.call-start = ((), (), s32[]{:S(2)}) async-start(), calls=%async_computation.3 | async-start | bytes 4456448 | tf_op jit(solution)/shard_map/reduce_scatter | solution.py:128
  125.0 0.9 copy-start.1
Sparse Core Ops, SparseCore 0:
  9.6 35.7 all-gather.1
  125.2 72.1 reduce-scatter.1
where the time goes:
time: 207 us; the launch traced here: 206 us
  waiting for transfers between devices  71.4 us (34%)
  blocking collectives  64.6 us (31%)
  matrix products  24.1 us (12%)
  local copies, waits for them, and re-layouts  15.1 us (7%)
  between operations  14.1 us (7%)
  other arithmetic  12.5 us (6%)
  loops' own time  4.02 us (2%)
    reduce_scatter x1, waiting for transfers between devices, local(): lax.psum_scatter(jnp.einsum('td,tn->dn', features, b_grad, preferred_elem...  70.7 us
    all_gather x1, blocking collectives, local(): lax.all_gather(keys, 'seq', axis=0, tiled=True)  26.4 us
    all_gather x1, blocking collectives, local(): lax.all_gather(b_local, 'seq', axis=0, tiled=True)  20.3 us
    all_to_all x1, blocking collectives, local(): lax.all_to_all(db_buffer.reshape(seq_count, shard_rows, state_width).asty...  18 us
    dot_general x4, matrix products, scores_of(): jnp.einsum('qhd,kd->qhk', query_heads, key_block, preferred_element_type=...  9.57 us
    dynamic_slice x4, local copies, waits for them, and re-layouts, block_sweep(): running, unused = lax.scan(advance, running, (stacked, offsets))  4.89 us
    unnamed x13, local copies, waits for them, and re-layouts  4.78 us
    dynamic_update_slice x2, local copies, waits for them, and re-layouts, advance_pair(): db_buffer = lax.dynamic_update_slice_in_dim(db_buffer, contrib, offset, 0)  4.53 us
  transfers between devices with their start and end apart: 2, of which 1 were waited for; matrix products, arithmetic and copies ran while one was open for 9% of the time, Pallas kernels for 0%

commit v1 on v0

v1 whole, which is shorter than its diff:
```python
import functools
import math

import jax
import jax.numpy as jnp
from jax import lax
from jax.experimental import pallas as pl
from jax.experimental.pallas import tpu as pltpu
from jax.sharding import PartitionSpec as P

NEG_FILL = -1e30
MESH = pl.DeviceIdType.MESH
CHUNKS = 4
BF16 = jnp.bfloat16
F32 = jnp.float32
NT = (((1,), (1,)), ((), ()))
TN = (((0,), (0,)), ((), ()))


def dot(a, b, dims=(((1,), (0,)), ((), ()))):
    return lax.dot_general(a, b, dims, preferred_element_type=F32)


def kernel(
    n_seq, n_kv, rows, width, heads,
    plan, q_ref, k_ref, c_ref, x_ref, w_ref,
    gc_ref, gw_ref,
    q_st, c_st, k_all, b_all, s_buf, top, tot, acc,
    wx, pbs, pbr, lt, db_all, dbs, snd, arr, db_own, dbg, fs, fr,
    k_sem, kr_sem, w_sem, wr_sem, pb_sem, x_sem, b_sem, br_sem, ds_sem, da_sem, dg_sem, f_sem, loc_sem,
):
    me, kv = lax.axis_index("seq"), lax.axis_index("kv")
    chips = n_seq // 2
    chip, core = me // 2, lax.rem(me, 2)
    sib = me + 1 - 2 * core
    per = n_seq // n_kv
    grp, pos = me // per, lax.rem(me, per)
    half = x_ref.shape[1]
    feat = half // per
    piece = half // 2
    step = piece // CHUNKS
    total = n_seq * n_kv
    wide = 2 * rows

    def blk(i, size=rows):
        return pl.ds(pl.multiple_of(i * size, size), size)

    def remote(src, dst, sems, i, j, dev):
        return pltpu.make_async_remote_copy(
            src_ref=src, dst_ref=dst, send_sem=sems.at[0, i], recv_sem=sems.at[1, j],
            device_id=dev, device_id_type=MESH,
        )

    barrier = pltpu.get_barrier_semaphore()
    flat = me * n_kv + kv

    def greet(d, carry):
        other = lax.rem(flat + d, total)
        pl.semaphore_signal(
            barrier, inc=1, device_id=(other // n_kv, lax.rem(other, n_kv)), device_id_type=MESH
        )
        return carry

    lax.fori_loop(1, total, greet, 0)
    pl.semaphore_wait(barrier, total - 1)

    def each(lo, hi, body):
        def run(i, carry):
            body(i)
            return carry

        lax.fori_loop(lo, hi, run, 0)

    def w_rows(i):
        return pl.ds(pl.multiple_of(core * piece + i * step, step), step)

    def w_copy(dk, i):
        other = lax.rem(kv + dk, n_kv)
        src = pl.ds(pl.multiple_of(other * half + core * piece + i * step, step), step)
        return remote(
            w_ref.at[0, src], wx.at[kv, w_rows(i)], w_sem, other * CHUNKS + i, kv * CHUNKS + i, (me, other)
        )

    def w_arrival(dk, i):
        other = lax.rem(kv + dk, n_kv)
        spot = wx.at[other, w_rows(i)]
        return remote(spot, spot, w_sem, other * CHUNKS + i, other * CHUNKS + i, (me, other))

    def w_relay(dk, i):
        other = lax.rem(kv + dk, n_kv)
        spot = wx.at[other, w_rows(i)]
        return remote(spot, spot, wr_sem, other * CHUNKS + i, other * CHUNKS + i, (sib, kv))

    for i in range(CHUNKS):
        for dk in range(1, n_kv):
            w_copy(dk, i).start()

    def direct(buf, sems, d):
        to = lax.rem(chip + d, chips)
        spot = buf.at[blk(me)]
        return remote(spot, spot, sems, to, chip, (2 * to + core, kv))

    def arrival(buf, sems, d):
        frm = lax.rem(chip + d, chips)
        spot = buf.at[blk(2 * frm + core)]
        return remote(spot, spot, sems, frm, frm, (2 * frm + core, kv))

    def relay(buf, sems, d):
        frm = lax.rem(chip + d, chips)
        spot = buf.at[blk(2 * frm + core)]
        return remote(spot, spot, sems, frm, frm, (sib, kv))

    def relayed(buf, sems, d):
        frm = lax.rem(chip + d, chips)
        spot = buf.at[blk(2 * frm + 1 - core)]
        return remote(spot, spot, sems, frm, frm, (sib, kv))

    def pass_on(buf, sems, rsems):
        def one(d):
            arrival(buf, sems, d).wait_recv()
            relay(buf, rsems, d).start()

        each(1, chips, one)
        each(0, chips, lambda d: relayed(buf, rsems, d).wait_recv())

    k_all[blk(me)] = k_ref[...]
    each(1, chips, lambda d: direct(k_all, k_sem, d).start())
    relay(k_all, kr_sem, 0).start()

    def x_copy(d):
        to = lax.rem(pos + d, per)
        cols = pl.ds(pl.multiple_of(to * feat, feat), feat)
        return remote(x_ref.at[:, cols], lt.at[blk(pos)], x_sem, to, pos, (grp * per + to, kv))

    def x_arrival(d):
        frm = lax.rem(pos + d, per)
        spot = lt.at[blk(frm)]
        return remote(spot, spot, x_sem, frm, frm, (grp * per + frm, kv))

    each(1, per, lambda d: x_copy(d).start())
    own_cols = pl.ds(pl.multiple_of(pos * feat, feat), feat)
    mine = pltpu.make_async_copy(x_ref.at[:, own_cols], lt.at[blk(pos)], loc_sem)
    mine.start()

    for h in range(heads):
        q_st[h * rows:(h + 1) * rows, :] = q_ref[:, h * width:(h + 1) * width]
        c_st[h * rows:(h + 1) * rows, :] = c_ref[:, h * width:(h + 1) * width]
    pbr[kv] = dot(x_ref[...], w_ref[0, pl.ds(pl.multiple_of(kv * half, half), half)])

    pass_on(k_all, k_sem, kr_sem)

    def w_forward(i):
        for dk in range(1, n_kv):
            w_arrival(dk, i).wait_recv()
            w_relay(dk, i).start()

    w_forward(0)

    own_plan = plan[me]
    row_id = lax.broadcasted_iota(jnp.int32, (heads * rows, rows), 0)
    col_id = lax.broadcasted_iota(jnp.int32, (heads * rows, rows), 1)
    gap = col_id - lax.rem(row_id, rows)

    def seen(block):
        return gap <= (own_plan - plan[block]) * rows

    score_scale = 1.0 / math.sqrt(width)
    student_scale = 2.0 / math.sqrt(rows * n_seq)
    top[...] = jnp.full_like(top, NEG_FILL)

    def scores(i):
        both = dot(q_st[...], k_all[blk(i, wide)], NT) * score_scale
        high = top[...]
        for t in range(2):
            part = jnp.where(seen(2 * i + t), both[:, t * rows:(t + 1) * rows], NEG_FILL)
            s_buf[i, :, t * rows:(t + 1) * rows] = part
            high = jnp.maximum(high, part)
        top[...] = high

    each(0, chips, scores)
    top[...] = jnp.broadcast_to(jnp.max(top[...], axis=1, keepdims=True), top.shape)
    for i in range(1, CHUNKS - 1):
        w_forward(i)
    tot[...] = jnp.zeros_like(tot)

    def weights(i):
        added = tot[...]
        for t in range(2):
            part = jnp.exp(s_buf[i, :, t * rows:(t + 1) * rows] - top[...])
            s_buf[i, :, t * rows:(t + 1) * rows] = part
            added = added + part
        tot[...] = added

    each(0, chips, weights)
    w_forward(CHUNKS - 1)
    tot[...] = jnp.broadcast_to(1.0 / jnp.sum(tot[...], axis=1, keepdims=True), tot.shape)

    def relayed_w(dk, i):
        other = lax.rem(kv + dk, n_kv)
        spot = wx.at[other, pl.ds(pl.multiple_of((1 - core) * piece + i * step, step), step)]
        return remote(spot, spot, wr_sem, other * CHUNKS + i, other * CHUNKS + i, (sib, kv))

    def pb_copy(dk):
        other = lax.rem(kv + dk, n_kv)
        return remote(pbs.at[other], pbr.at[kv], pb_sem, other, kv, (me, other))

    def pb_arrival(dk):
        other = lax.rem(kv + dk, n_kv)
        return remote(pbr.at[other], pbr.at[other], pb_sem, other, other, (me, other))

    for dk in range(1, n_kv):
        other = lax.rem(kv + dk, n_kv)
        for i in range(CHUNKS):
            relayed_w(dk, i).wait_recv()
        pbs[other] = dot(x_ref[...], wx[other])
        pb_copy(dk).start()
    for dk in range(1, n_kv):
        pb_arrival(dk).wait_recv()
    b_sum = pbr[0]
    for g in range(1, n_kv):
        b_sum = b_sum + pbr[g]
    b_all[blk(me)] = b_sum.astype(BF16)
    each(1, chips, lambda d: direct(b_all, b_sem, d).start())
    relay(b_all, br_sem, 0).start()
    pass_on(b_all, b_sem, br_sem)

    acc[...] = jnp.zeros_like(acc)

    def to_sib(i):
        return remote(
            db_all.at[i, pl.ds(pl.multiple_of((1 - core) * rows, rows), rows)], dbs.at[i], ds_sem, i, i, (sib, kv)
        )

    def to_owner(i):
        return remote(snd.at[i], arr.at[chip], da_sem, i, chip, (2 * i + core, kv))

    def from_chip(i):
        return remote(arr.at[i], arr.at[i], da_sem, i, i, (2 * i + core, kv))

    def joined(i):
        to_sib(i).wait_recv()
        return db_all[i, pl.ds(pl.multiple_of(core * rows, rows), rows)] + dbs[i]

    def send_on(i):
        snd[i] = joined(i).astype(BF16)
        to_owner(i).start()

    def residuals(t):
        i = lax.rem(chip + 1 + t, chips)
        b_two = b_all[blk(i, wide)]
        c_rows = c_st[...]
        student = dot(c_rows, b_two, NT)
        parts = []
        for u in range(2):
            part = student_scale * student[:, u * rows:(u + 1) * rows] - (
                s_buf[i, :, u * rows:(u + 1) * rows] * tot[...]
            )
            parts.append(jnp.where(seen(2 * i + u), part, 0.0).astype(BF16))
        resid = jnp.concatenate(parts, axis=1)
        db_all[i] = dot(resid, c_rows, TN)
        to_sib(i).start()
        acc[...] += dot(resid, b_two)

        @pl.when(t > 0)
        def _():
            send_on(lax.rem(chip + t, chips))

    each(0, chips, residuals)
    db_own[...] = joined(chip)
    for h in range(heads):
        gc_ref[:, h * width:(h + 1) * width] = acc[h * rows:(h + 1) * rows, :].astype(BF16)

    def take(d):
        i = lax.rem(chip + d, chips)
        from_chip(i).wait_recv()
        db_own[...] += arr[i].astype(F32)

    each(1, chips, take)
    dbg[kv, blk(pos)] = db_own[...].astype(BF16)

    def dg_target(d):
        idx = lax.rem(pos * n_kv + kv + d, per * n_kv)
        return idx, idx // n_kv, lax.rem(idx, n_kv)

    def dg_copy(d):
        idx, p, g = dg_target(d)
        spot = dbg.at[kv, blk(pos)]
        return remote(spot, spot, dg_sem, idx, pos * n_kv + kv, (grp * per + p, g))

    def dg_arrival(d):
        idx, p, g = dg_target(d)
        spot = dbg.at[g, blk(p)]
        return remote(spot, spot, dg_sem, idx, idx, (grp * per + p, g))

    each(1, per * n_kv, lambda d: dg_copy(d).start())
    each(1, per, lambda d: x_arrival(d).wait_recv())
    mine.wait()
    each(1, per * n_kv, lambda d: dg_arrival(d).wait_recv())

    owner = per * kv + pos

    def f_copy(g):
        return remote(fs.at[g], fr.at[grp], f_sem, g, grp, (owner, g))

    def f_arrival(h):
        return remote(fr.at[h], fr.at[h], f_sem, h, h, (h * per + pos, grp))

    for dk in range(n_kv):
        g = lax.rem(kv + 1 + dk, n_kv)
        part = dot(lt[...], dbg[g], TN)
        if dk < n_kv - 1:
            fs[g] = part.astype(BF16)
            f_copy(g).start()
        else:
            @pl.when(grp == kv)
            def _():
                gw_ref[0] = part

            @pl.when(grp != kv)
            def _():
                fs[g] = part.astype(BF16)
                f_copy(g).start()
                gw_ref[0] = jnp.zeros_like(part)

    for h in range(n_kv):
        @pl.when(jnp.logical_or(grp != kv, grp != h))
        def _():
            f_arrival(h).wait_recv()
            gw_ref[0] += fr[h].astype(F32)

    for i in range(CHUNKS):
        for dk in range(1, n_kv):
            w_copy(dk, i).wait_send()
            w_relay(dk, i).wait_send()
    for dk in range(1, n_kv):
        pb_copy(dk).wait_send()

    def drain(d):
        direct(k_all, k_sem, d).wait_send()
        direct(b_all, b_sem, d).wait_send()
        to_owner(lax.rem(chip + d, chips)).wait_send()

    def drain_all(d):
        relay(k_all, kr_sem, d).wait_send()
        relay(b_all, br_sem, d).wait_send()
        to_sib(d).wait_send()

    each(1, chips, drain)
    each(0, chips, drain_all)
    each(1, per, lambda d: x_copy(d).wait_send())
    each(1, per * n_kv, lambda d: dg_copy(d).wait_send())
    for g in range(n_kv):
        @pl.when(jnp.logical_or(grp != kv, kv != g))
        def _():
            f_copy(g).wait_send()


def local(n_seq, n_kv, plan, queries, keys, student_c, layer_input, b_weight):
    rows, width = keys.shape
    heads = queries.shape[1] // width
    half = layer_input.shape[1]
    depth = b_weight.shape[1]
    feat = depth // n_seq
    chips = n_seq // 2
    per = n_seq // n_kv
    stack = heads * rows
    vmem = pltpu.VMEM

    def pair(count):
        return pltpu.SemaphoreType.DMA((2, count))

    whole = pl.BlockSpec(memory_space=pltpu.VMEM)
    return pl.pallas_call(
        functools.partial(kernel, n_seq, n_kv, rows, width, heads),
        out_shape=(
            jax.ShapeDtypeStruct(queries.shape, BF16),
            jax.ShapeDtypeStruct((1, feat, width), F32),
        ),
        in_specs=[pl.BlockSpec(memory_space=pltpu.SMEM)] + [whole] * 5,
        out_specs=(whole, whole),
        scratch_shapes=[
            vmem((stack, width), BF16), vmem((stack, width), BF16),
            vmem((n_seq * rows, width), BF16), vmem((n_seq * rows, width), BF16),
            vmem((chips, stack, 2 * rows), F32),
            vmem((stack, rows), F32), vmem((stack, rows), F32), vmem((stack, width), F32),
            vmem((n_kv, half, width), BF16),
            vmem((n_kv, rows, width), F32), vmem((n_kv, rows, width), F32),
            vmem((per * rows, feat), BF16),
            vmem((chips, 2 * rows, width), F32), vmem((chips, rows, width), F32),
            vmem((chips, rows, width), BF16), vmem((chips, rows, width), BF16),
            vmem((rows, width), F32),
            vmem((n_kv, per * rows, width), BF16),
            vmem((n_kv, feat, width), BF16), vmem((n_kv, feat, width), BF16),
            pair(chips), pair(chips), pair(n_kv * CHUNKS), pair(n_kv * CHUNKS), pair(n_kv),
            pair(per), pair(chips), pair(chips), pair(chips), pair(chips), pair(per * n_kv),
            pair(n_kv), pltpu.SemaphoreType.DMA,
        ],
        compiler_params=pltpu.CompilerParams(
            collective_id=0, has_side_effects=True, vmem_limit_bytes=56 * 2**20
        ),
        name="ssm_grad",
    )(plan, queries, keys, student_c, layer_input, b_weight)


def solution(mesh):
    in_specs = (
        P(),
        P("seq", "kv"),
        P("seq", "kv"),
        P("seq", "kv"),
        P("seq", "kv"),
        P("kv", None, None),
    )
    out_specs = (P("seq", "kv"), P("kv", "seq", None))
    body = functools.partial(local, mesh.shape["seq"], mesh.shape["kv"])
    return jax.shard_map(body, mesh=mesh, in_specs=in_specs, out_specs=out_specs, check_vma=False)
```

time: 207 us -> 73.8 us (0.36)
  waiting for transfers between devices: 71.4 us -> 0 us
  Pallas kernels: 0 us -> 69.8 us
  blocking collectives: 64.6 us -> 0 us
  matrix products: 24.1 us -> 0 us
  between operations: 14.1 us -> 0.64 us
  other arithmetic: 12.5 us -> 0 us
  local copies, waits for them, and re-layouts: 15.1 us -> 3.24 us
  loops' own time: 4.02 us -> 0 us
    reduce_scatter x1 -> x0, waiting for transfers between devices: 70.7 us -> none  [local(): lax.psum_scatter(jnp.einsum('td,tn->dn', features, b_grad, preferred_elem...]
    pallas_call x0 -> x1, Pallas kernels: none -> 69.8 us  [local(): pl.pallas_call(functools.partial(kernel, n_seq, n_kv, rows, width, heads)...]
    all_gather x2 -> x0, blocking collectives: 46.6 us -> none  [the longest x1 26.4 us: local(): lax.all_gather(keys, 'seq', axis=0, tiled=True)]
    dot_general x12 -> x0, matrix products: 24.1 us -> none  [the longest x4 9.57 us: scores_of(): jnp.einsum('qhd,kd->qhk', query_heads, key_block, preferred_element_type=...]
    all_to_all x1 -> x0, blocking collectives: 18 us -> none  [local(): lax.all_to_all(db_buffer.reshape(seq_count, shard_rows, state_width).asty...]
    reduce_sum x8 -> x0, other arithmetic: 5.39 us -> none  [the longest x2 4.24 us: stats_step(): jnp.sum(weights, axis=-1)]
    dynamic_slice x4 -> x0, local copies, waits for them, and re-layouts: 4.89 us -> none  [block_sweep(): running, unused = lax.scan(advance, running, (stacked, offsets))]
    dynamic_update_slice x2 -> x0, local copies, waits for them, and re-layouts: 4.53 us -> none  [advance_pair(): db_buffer = lax.dynamic_update_slice_in_dim(db_buffer, contrib, offset, 0)]
  transfers between devices with their start and end apart: 2 -> 0, of which waited for: 1 -> 0; matrix products, arithmetic and copies ran while one was open for 9% -> 0% of each run, Pallas kernels for 0% -> 0%
where the time goes in v1:
time: 73.8 us; the launch traced here: 73.7 us
  Pallas kernels  69.8 us (95%)
  local copies, waits for them, and re-layouts  3.24 us (4%)
    pallas_call x1, Pallas kernels, local(): pl.pallas_call(functools.partial(kernel, n_seq, n_kv, rows, width, heads)...  69.8 us
    unnamed x2, local copies, waits for them, and re-layouts  3.24 us

profile of v1, /device:TPU:0, one launch (start us, length us, event | category | flops | bytes accessed | tf_op | source)
XLA Modules:
  0.0 73.7 jit_solution(5957892081107888439)
XLA Ops:
  0.6 69.8 %ssm_grad.1 = (bf16[128,512]{1,0:T(8,128)(2,1)}, f32[1,512,128]{2,1,0:T(8,128)}) custom-call(s32[16]{0:T(128)} %plan.1, bf16[128,512]{1,0:T(8,128)(2,1)} %q_ref.1, bf16[128,128]{1,0:T(8,128)(2,1)} %k_ref.1, bf16[128,512]{1,0:T(8,128)(2,1)} %c_ref.1, bf16[128,4096]{1,0:T(8,128)(2,1)} %x_ref.1, bf16[1,8192,128]{2,1,0:T(8,128)(2,1)} %w_ref.1), custom_call_target="tpu_custom_call" | custom-call | tf_op jit(solution)/shard_map/ssm_grad/pallas_call | solution.py:373
  70.4 1.6 %copy.10 = bf16[128,512]{1,0:T(8,128)(2,1)} copy(bf16[128,512]{1,0:T(8,128)(2,1)} %get-tuple-element.4) | data formatting | bytes 262144
  72.0 1.7 %copy.11 = f32[1,512,128]{2,1,0:T(8,128)} copy(f32[1,512,128]{2,1,0:T(8,128)} %get-tuple-element.5) | data formatting | bytes 524288

commit v2 on v1

v2 whole, which is shorter than its diff:
```python
import functools
import math

import jax
import jax.numpy as jnp
from jax import lax
from jax.experimental import pallas as pl
from jax.experimental.pallas import tpu as pltpu
from jax.sharding import PartitionSpec as P

NEG_FILL = -1e30
MESH = pl.DeviceIdType.MESH
CHUNKS = 4
BF16 = jnp.bfloat16
F32 = jnp.float32
NT = (((1,), (1,)), ((), ()))
TN = (((0,), (0,)), ((), ()))


def dot(a, b, dims=(((1,), (0,)), ((), ()))):
    return lax.dot_general(a, b, dims, preferred_element_type=F32)


def kernel(
    n_seq, n_kv, rows, width, heads,
    plan, q_ref, k_ref, c_ref, x_any, w_any,
    gc_ref, gw_ref,
    x_ref, wv, q_t, c_t, c_st, k_all, b_all, s_buf, top, tot, acc,
    wx, pbs, pbr, lt, lt_t, db_all, dbs, snd, arr, db_own, dbg, fs, fr,
    k_sem, kr_sem, w_sem, wr_sem, pb_sem, x_sem, b_sem, br_sem, ds_sem, da_sem, dg_sem, dr_sem, f_sem, loc_sem,
):
    me, kv = lax.axis_index("seq"), lax.axis_index("kv")
    chips = n_seq // 2
    chip, core = me // 2, lax.rem(me, 2)
    sib = me + 1 - 2 * core
    per = n_seq // n_kv
    grp, pos = me // per, lax.rem(me, per)
    half = x_ref.shape[1]
    feat = half // per
    piece = half // 2
    step = piece // CHUNKS
    total = n_seq * n_kv
    wide = 2 * rows

    def blk(i, size=rows):
        return pl.ds(pl.multiple_of(i * size, size), size)

    def remote(src, dst, sems, i, j, dev):
        return pltpu.make_async_remote_copy(
            src_ref=src, dst_ref=dst, send_sem=sems.at[0, i], recv_sem=sems.at[1, j],
            device_id=dev, device_id_type=MESH,
        )

    barrier = pltpu.get_barrier_semaphore()
    flat = me * n_kv + kv

    def greet(d, carry):
        other = lax.rem(flat + d, total)
        pl.semaphore_signal(
            barrier, inc=1, device_id=(other // n_kv, lax.rem(other, n_kv)), device_id_type=MESH
        )
        return carry

    lax.fori_loop(1, total, greet, 0)
    own_half = pl.ds(pl.multiple_of(kv * half, half), half)
    load_x = pltpu.make_async_copy(x_any, x_ref, loc_sem.at[0])
    load_w = pltpu.make_async_copy(w_any.at[0, own_half], wv, loc_sem.at[1])
    load_x.start()
    load_w.start()
    pl.semaphore_wait(barrier, total - 1)

    def each(lo, hi, body):
        def run(i, carry):
            body(i)
            return carry

        lax.fori_loop(lo, hi, run, 0)

    def w_spot(other, part, i):
        return wx.at[other, pl.ds(pl.multiple_of(part * piece + i * step, step), step)]

    def w_copy(dk, i):
        other = lax.rem(kv + dk, n_kv)
        src = pl.ds(pl.multiple_of(other * half + core * piece + i * step, step), step)
        return remote(
            w_any.at[0, src], w_spot(kv, core, i), w_sem, other * CHUNKS + i, kv * CHUNKS + i, (me, other)
        )

    def w_hop(dk, i, part, sems, to):
        other = lax.rem(kv + dk, n_kv)
        spot = w_spot(other, part, i)
        return remote(spot, spot, sems, other * CHUNKS + i, other * CHUNKS + i, (to, kv))

    for i in range(CHUNKS):
        for dk in range(1, n_kv):
            w_copy(dk, i).start()

    def direct(buf, sems, d):
        to = lax.rem(chip + d, chips)
        spot = buf.at[blk(me)]
        return remote(spot, spot, sems, to, chip, (2 * to + core, kv))

    def arrival(buf, sems, d):
        frm = lax.rem(chip - d + chips, chips)
        spot = buf.at[blk(2 * frm + core)]
        return remote(spot, spot, sems, frm, frm, (2 * frm + core, kv))

    def relay(buf, sems, d):
        frm = lax.rem(chip - d + chips, chips)
        spot = buf.at[blk(2 * frm + core)]
        return remote(spot, spot, sems, frm, frm, (sib, kv))

    def relayed(buf, sems, d):
        frm = lax.rem(chip - d + chips, chips)
        spot = buf.at[blk(2 * frm + 1 - core)]
        return remote(spot, spot, sems, frm, frm, (sib, kv))

    def pass_on(buf, sems, rsems):
        def one(d):
            arrival(buf, sems, d).wait_recv()
            relay(buf, rsems, d).start()

        each(1, chips, one)
        each(0, chips, lambda d: relayed(buf, rsems, d).wait_recv())

    k_all[blk(me)] = k_ref[...]
    each(1, chips, lambda d: direct(k_all, k_sem, d).start())
    relay(k_all, kr_sem, 0).start()

    def x_copy(d):
        to = lax.rem(pos + d, per)
        cols = pl.ds(pl.multiple_of(to * feat, feat), feat)
        return remote(x_any.at[:, cols], lt.at[blk(pos)], x_sem, to, pos, (grp * per + to, kv))

    def x_arrival(d):
        frm = lax.rem(pos + d, per)
        spot = lt.at[blk(frm)]
        return remote(spot, spot, x_sem, frm, frm, (grp * per + frm, kv))

    each(1, per, lambda d: x_copy(d).start())
    own_cols = pl.ds(pl.multiple_of(pos * feat, feat), feat)
    mine = pltpu.make_async_copy(x_any.at[:, own_cols], lt.at[blk(pos)], loc_sem.at[2])
    mine.start()
    for h in range(heads):
        cols = slice(h * width, (h + 1) * width)
        q_t[:, h * rows:(h + 1) * rows] = q_ref[:, cols].astype(F32).T.astype(BF16)
        c_t[:, h * rows:(h + 1) * rows] = c_ref[:, cols].astype(F32).T.astype(BF16)
        c_st[h * rows:(h + 1) * rows, :] = c_ref[:, cols]
    load_x.wait()
    load_w.wait()
    pbr[kv] = dot(x_ref[...], wv[...])

    def w_forward(i):
        for dk in range(1, n_kv):
            w_hop(dk, i, core, w_sem, me).wait_recv()
            w_hop(dk, i, core, wr_sem, sib).start()

    pass_on(k_all, k_sem, kr_sem)
    w_forward(0)

    own_plan = plan[me]
    row_id = lax.broadcasted_iota(jnp.int32, (rows, heads * rows), 1)
    key_id = lax.broadcasted_iota(jnp.int32, (rows, heads * rows), 0)
    gap = key_id - lax.rem(row_id, rows)

    def seen(block):
        return gap <= (own_plan - plan[block]) * rows

    score_scale = 1.0 / math.sqrt(width)
    student_scale = 2.0 / math.sqrt(rows * n_seq)
    top[...] = jnp.full_like(top, NEG_FILL)

    def fold(part):
        return part.reshape(rows // 8, 8, heads * rows)

    def scores(i):
        both = dot(k_all[blk(i, wide)], q_t[...]) * score_scale
        high = top[...]
        for t in range(2):
            part = jnp.where(seen(2 * i + t), both[t * rows:(t + 1) * rows], NEG_FILL)
            s_buf[i, t * rows:(t + 1) * rows] = part
            high = jnp.maximum(high, jnp.max(fold(part), axis=0))
        top[...] = high

    each(0, chips, scores)
    w_forward(1)
    top[...] = jnp.broadcast_to(jnp.max(top[...], axis=0, keepdims=True), top.shape)

    def weights(i):
        added = tot[...]
        for t in range(2):
            part = jnp.exp(s_buf[i, t * rows:(t + 1) * rows] - top[0:1])
            s_buf[i, t * rows:(t + 1) * rows] = part
            added = added + jnp.sum(fold(part), axis=0)
        tot[...] = added

    tot[...] = jnp.zeros_like(tot)
    each(0, chips, weights)
    tot[...] = jnp.broadcast_to(1.0 / jnp.sum(tot[...], axis=0, keepdims=True), tot.shape)
    for i in range(2, CHUNKS):
        w_forward(i)

    def pb_copy(dk):
        other = lax.rem(kv + dk, n_kv)
        return remote(pbs.at[other], pbr.at[kv], pb_sem, other, kv, (me, other))

    def pb_arrival(dk):
        other = lax.rem(kv + dk, n_kv)
        return remote(pbr.at[other], pbr.at[other], pb_sem, other, other, (me, other))

    for dk in range(1, n_kv):
        other = lax.rem(kv + dk, n_kv)
        for i in range(CHUNKS):
            w_hop(dk, i, 1 - core, wr_sem, sib).wait_recv()
        pbs[other] = dot(x_ref[...], wx[other])
        pb_copy(dk).start()
    for dk in range(1, n_kv):
        pb_arrival(dk).wait_recv()
    b_sum = pbr[0]
    for g in range(1, n_kv):
        b_sum = b_sum + pbr[g]
    b_all[blk(me)] = b_sum.astype(BF16)
    each(1, chips, lambda d: direct(b_all, b_sem, d).start())
    relay(b_all, br_sem, 0).start()

    acc[...] = jnp.zeros_like(acc)

    def to_sib(i):
        return remote(
            db_all.at[i, pl.ds(pl.multiple_of((1 - core) * rows, rows), rows)], dbs.at[i], ds_sem, i, i, (sib, kv)
        )

    def to_owner(i):
        return remote(snd.at[i], arr.at[chip], da_sem, i, chip, (2 * i + core, kv))

    def from_chip(i):
        return remote(arr.at[i], arr.at[i], da_sem, i, i, (2 * i + core, kv))

    def joined(i):
        to_sib(i).wait_recv()
        return db_all[i, pl.ds(pl.multiple_of(core * rows, rows), rows)] + dbs[i]

    def send_on(i):
        snd[i] = joined(i).astype(BF16)
        to_owner(i).start()

    def residuals(t):
        i = lax.rem(chip - t + chips, chips)

        @pl.when(t < chips - 1)
        def _():
            arrival(b_all, b_sem, t + 1).wait_recv()
            relay(b_all, br_sem, t + 1).start()

        relayed(b_all, br_sem, t).wait_recv()
        b_two = b_all[blk(i, wide)]
        student = dot(b_two, c_t[...])
        parts = []
        for u in range(2):
            part = student_scale * student[u * rows:(u + 1) * rows] - (
                s_buf[i, u * rows:(u + 1) * rows] * tot[0:1]
            )
            parts.append(jnp.where(seen(2 * i + u), part, 0.0).astype(BF16))
        resid = jnp.concatenate(parts, axis=0)
        db_all[i] = dot(resid, c_st[...])
        to_sib(i).start()
        acc[...] += dot(b_two, resid, TN)

        @pl.when(t > 1)
        def _():
            send_on(lax.rem(chip - t + 1 + chips, chips))

    each(0, chips, residuals)
    send_on(lax.rem(chip + 1, chips))
    db_own[...] = joined(chip)
    for h in range(heads):
        gc_ref[:, h * width:(h + 1) * width] = acc[:, h * rows:(h + 1) * rows].T.astype(BF16)
    each(1, per, lambda d: x_arrival(d).wait_recv())
    mine.wait()

    def turn(p):
        lt_t[:, blk(p)] = lt[blk(p)].T

    each(0, per, turn)

    def take(d):
        i = lax.rem(chip + d, chips)
        from_chip(i).wait_recv()
        db_own[...] += arr[i].astype(F32)

    each(1, chips, take)
    dbg[kv, blk(pos)] = db_own[...].astype(BF16)

    count = per // 2 * n_kv
    spot_own = pos // 2 * n_kv + kv

    def dg_at(idx, which):
        return dbg.at[lax.rem(idx, n_kv), blk(2 * (idx // n_kv) + which)]

    def dg_copy(d):
        to = lax.rem(spot_own + d, count)
        spot = dg_at(spot_own, core)
        return remote(spot, spot, dg_sem, to, spot_own, (grp * per + 2 * (to // n_kv) + core, lax.rem(to, n_kv)))

    def dg_hop(d, sems, which):
        frm = lax.rem(spot_own - d + count, count)
        spot = dg_at(frm, which)
        return remote(spot, spot, sems, frm, frm, (sib, kv))

    each(1, count, lambda d: dg_copy(d).start())
    dg_hop(0, dr_sem, core).start()

    def dg_pass(d):
        dg_hop(d, dg_sem, core).wait_recv()
        dg_hop(d, dr_sem, core).start()

    each(1, count, dg_pass)
    each(0, count, lambda d: dg_hop(d, dr_sem, 1 - core).wait_recv())

    owner = per * kv + pos

    def f_copy(g):
        return remote(fs.at[g], fr.at[grp], f_sem, g, grp, (owner, g))

    def f_arrival(h):
        return remote(fr.at[h], fr.at[h], f_sem, h, h, (h * per + pos, grp))

    for dk in range(n_kv):
        g = lax.rem(kv + 1 + dk, n_kv)
        part = dot(lt_t[...], dbg[g])
        if dk < n_kv - 1:
            fs[g] = part.astype(BF16)
            f_copy(g).start()
        else:
            @pl.when(grp == kv)
            def _():
                gw_ref[0] = part

            @pl.when(grp != kv)
            def _():
                fs[g] = part.astype(BF16)
                f_copy(g).start()
                gw_ref[0] = jnp.zeros_like(part)

    for h in range(n_kv):
        @pl.when(jnp.logical_or(grp != kv, grp != h))
        def _():
            f_arrival(h).wait_recv()
            gw_ref[0] += fr[h].astype(F32)

    for i in range(CHUNKS):
        for dk in range(1, n_kv):
            w_copy(dk, i).wait_send()
            w_hop(dk, i, core, wr_sem, sib).wait_send()
    for dk in range(1, n_kv):
        pb_copy(dk).wait_send()

    def drain(d):
        direct(k_all, k_sem, d).wait_send()
        direct(b_all, b_sem, d).wait_send()
        to_owner(lax.rem(chip + d, chips)).wait_send()

    def drain_all(d):
        relay(k_all, kr_sem, d).wait_send()
        relay(b_all, br_sem, d).wait_send()
        to_sib(d).wait_send()

    each(1, chips, drain)
    each(0, chips, drain_all)
    each(1, per, lambda d: x_copy(d).wait_send())
    each(1, count, lambda d: dg_copy(d).wait_send())
    each(0, count, lambda d: dg_hop(d, dr_sem, core).wait_send())
    for g in range(n_kv):
        @pl.when(jnp.logical_or(grp != kv, kv != g))
        def _():
            f_copy(g).wait_send()


def local(n_seq, n_kv, plan, queries, keys, student_c, layer_input, b_weight):
    rows, width = keys.shape
    heads = queries.shape[1] // width
    half = layer_input.shape[1]
    depth = b_weight.shape[1]
    feat = depth // n_seq
    chips = n_seq // 2
    per = n_seq // n_kv
    stack = heads * rows
    vmem = pltpu.VMEM

    def pair(count):
        return pltpu.SemaphoreType.DMA((2, count))

    whole = pl.BlockSpec(memory_space=pltpu.VMEM)
    return pl.pallas_call(
        functools.partial(kernel, n_seq, n_kv, rows, width, heads),
        out_shape=(
            jax.ShapeDtypeStruct(queries.shape, BF16),
            jax.ShapeDtypeStruct((1, feat, width), F32),
        ),
        in_specs=[pl.BlockSpec(memory_space=pltpu.SMEM)] + [whole] * 3 + [pl.BlockSpec(memory_space=pl.ANY)] * 2,
        out_specs=(whole, whole),
        scratch_shapes=[
            vmem((rows, half), BF16), vmem((half, width), BF16),
            vmem((width, stack), BF16), vmem((width, stack), BF16), vmem((stack, width), BF16),
            vmem((n_seq * rows, width), BF16), vmem((n_seq * rows, width), BF16),
            vmem((chips, 2 * rows, stack), F32),
            vmem((8, stack), F32), vmem((8, stack), F32), vmem((width, stack), F32),
            vmem((n_kv, half, width), BF16),
            vmem((n_kv, rows, width), F32), vmem((n_kv, rows, width), F32),
            vmem((per * rows, feat), BF16), vmem((feat, per * rows), BF16),
            vmem((chips, 2 * rows, width), F32), vmem((chips, rows, width), F32),
            vmem((chips, rows, width), BF16), vmem((chips, rows, width), BF16),
            vmem((rows, width), F32),
            vmem((n_kv, per * rows, width), BF16),
            vmem((n_kv, feat, width), BF16), vmem((n_kv, feat, width), BF16),
            pair(chips), pair(chips), pair(n_kv * CHUNKS), pair(n_kv * CHUNKS), pair(n_kv),
            pair(per), pair(chips), pair(chips), pair(chips), pair(chips), pair(per // 2 * n_kv),
            pair(per // 2 * n_kv), pair(n_kv), pltpu.SemaphoreType.DMA((3,)),
        ],
        compiler_params=pltpu.CompilerParams(
            collective_id=0, has_side_effects=True, vmem_limit_bytes=56 * 2**20
        ),
        name="ssm_grad",
    )(plan, queries, keys, student_c, layer_input, b_weight)


def solution(mesh):
    in_specs = (
        P(),
        P("seq", "kv"),
        P("seq", "kv"),
        P("seq", "kv"),
        P("seq", "kv"),
        P("kv", None, None),
    )
    out_specs = (P("seq", "kv"), P("kv", "seq", None))
    body = functools.partial(local, mesh.shape["seq"], mesh.shape["kv"])
    return jax.shard_map(body, mesh=mesh, in_specs=in_specs, out_specs=out_specs, check_vma=False)
```

time: 73.8 us -> 66.9 us (0.907)
  Pallas kernels: 69.8 us -> 62.9 us
    pallas_call x1, Pallas kernels: 69.8 us -> 62.9 us  [local(): pl.pallas_call(functools.partial(kernel, n_seq, n_kv, rows, width, heads)...]
where the time goes in v2:
time: 66.9 us; the launch traced here: 66.7 us
  Pallas kernels  62.9 us (94%)
  local copies, waits for them, and re-layouts  3.24 us (5%)
    pallas_call x1, Pallas kernels, local(): pl.pallas_call(functools.partial(kernel, n_seq, n_kv, rows, width, heads)...  62.9 us
    unnamed x2, local copies, waits for them, and re-layouts  3.24 us

profile of v2, /device:TPU:0, one launch (start us, length us, event | category | flops | bytes accessed | tf_op | source)
XLA Modules:
  0.0 66.7 jit_solution(2972981374650385465)
XLA Ops:
  0.6 62.9 %ssm_grad.1 = (bf16[128,512]{1,0:T(8,128)(2,1)}, f32[1,512,128]{2,1,0:T(8,128)}) custom-call(s32[16]{0:T(128)} %plan.1, bf16[128,512]{1,0:T(8,128)(2,1)} %q_ref.1, bf16[128,128]{1,0:T(8,128)(2,1)} %k_ref.1, bf16[128,512]{1,0:T(8,128)(2,1)} %c_ref.1, bf16[128,4096]{1,0:T(8,128)(2,1)} %x_any.1, bf16[1,8192,128]{2,1,0:T(8,128)(2,1)} %w_any.1), custom_call_target="tpu_custom_call" | custom-call | tf_op jit(solution)/shard_map/ssm_grad/pallas_call | solution.py:394
  63.5 1.6 %copy.10 = bf16[128,512]{1,0:T(8,128)(2,1)} copy(bf16[128,512]{1,0:T(8,128)(2,1)} %get-tuple-element.4) | data formatting | bytes 262144
  65.1 1.7 %copy.11 = f32[1,512,128]{2,1,0:T(8,128)} copy(f32[1,512,128]{2,1,0:T(8,128)} %get-tuple-element.5) | data formatting | bytes 524288

commit v3 on v2

--- a/solution.py
+++ b/solution.py
@@ -11,6 +11,7 @@
 NEG_FILL = -1e30
 MESH = pl.DeviceIdType.MESH
 CHUNKS = 4
+PARTS = 4
 BF16 = jnp.bfloat16
 F32 = jnp.float32
 NT = (((1,), (1,)), ((), ()))
@@ -26,8 +27,8 @@
     plan, q_ref, k_ref, c_ref, x_any, w_any,
     gc_ref, gw_ref,
     x_ref, wv, q_t, c_t, c_st, k_all, b_all, s_buf, top, tot, acc,
-    wx, pbs, pbr, lt, lt_t, db_all, dbs, snd, arr, db_own, dbg, fs, fr,
-    k_sem, kr_sem, w_sem, wr_sem, pb_sem, x_sem, b_sem, br_sem, ds_sem, da_sem, dg_sem, dr_sem, f_sem, loc_sem,
+    wx, pbs, pbr, lt, lt_t, db_all, dbs, snd, arr, db_own, dbg, fs, fx, fr,
+    k_sem, kr_sem, w_sem, wr_sem, pb_sem, x_sem, b_sem, br_sem, ds_sem, da_sem, dg_sem, dr_sem, f_sem, fa_sem, loc_sem,
 ):
     me, kv = lax.axis_index("seq"), lax.axis_index("kv")
     chips = n_seq // 2
@@ -317,36 +318,65 @@
     each(1, count, dg_pass)
     each(0, count, lambda d: dg_hop(d, dr_sem, 1 - core).wait_recv())
 
-    owner = per * kv + pos
-
-    def f_copy(g):
-        return remote(fs.at[g], fr.at[grp], f_sem, g, grp, (owner, g))
-
-    def f_arrival(h):
-        return remote(fr.at[h], fr.at[h], f_sem, h, h, (h * per + pos, grp))
-
-    for dk in range(n_kv):
-        g = lax.rem(kv + 1 + dk, n_kv)
-        part = dot(lt_t[...], dbg[g])
-        if dk < n_kv - 1:
-            fs[g] = part.astype(BF16)
-            f_copy(g).start()
-        else:
-            @pl.when(grp == kv)
+    part_rows = feat // PARTS
+
+    def f_rows(u):
+        return pl.ds(u * part_rows, part_rows)
+
+    def f_cross(g, u):
+        return remote(
+            fs.at[g, f_rows(u)], fx.at[kv, f_rows(u)], f_sem, g * PARTS + u, kv * PARTS + u, (me, g)
+        )
+
+    def f_crossed(g, u):
+        spot = fx.at[g, f_rows(u)]
+        return remote(spot, spot, f_sem, g * PARTS + u, g * PARTS + u, (me, g))
+
+    def f_along(buf, k, u):
+        return remote(
+            buf.at[k, f_rows(u)], fr.at[grp, f_rows(u)], fa_sem, k * PARTS + u, grp * PARTS + u, (per * k + pos, kv)
+        )
+
+    def f_arrival(h, u):
+        spot = fr.at[h, f_rows(u)]
+        return remote(spot, spot, fa_sem, h * PARTS + u, h * PARTS + u, (h * per + pos, kv))
+
+    for u in range(PARTS):
+        for dk in range(1, n_kv):
+            g = lax.rem(kv + dk, n_kv)
+            fs[g, f_rows(u)] = dot(lt_t[f_rows(u)], dbg[g]).astype(BF16)
+            f_cross(g, u).start()
+    part = dot(lt_t[...], dbg[kv])
+
+    @pl.when(grp == kv)
+    def _():
+        gw_ref[0] = part
+
+    @pl.when(grp != kv)
+    def _():
+        fs[kv] = part.astype(BF16)
+        for u in range(PARTS):
+            f_along(fs, kv, u).start()
+        gw_ref[0] = jnp.zeros_like(part)
+
+    for u in range(PARTS):
+        for dk in range(1, n_kv):
+            g = lax.rem(kv + dk, n_kv)
+            f_crossed(g, u).wait_recv()
+
+            @pl.when(grp == g)
             def _():
-                gw_ref[0] = part
-
-            @pl.when(grp != kv)
+                gw_ref[0, f_rows(u)] += fx[g, f_rows(u)].astype(F32)
+
+            @pl.when(grp != g)
             def _():
-                fs[g] = part.astype(BF16)
-                f_copy(g).start()
-                gw_ref[0] = jnp.zeros_like(part)
-
-    for h in range(n_kv):
-        @pl.when(jnp.logical_or(grp != kv, grp != h))
-        def _():
-            f_arrival(h).wait_recv()
-            gw_ref[0] += fr[h].astype(F32)
+                f_along(fx, g, u).start()
+
+    for u in range(PARTS):
+        for dk in range(1, n_kv):
+            h = lax.rem(grp + dk, n_kv)
+            f_arrival(h, u).wait_recv()
+            gw_ref[0, f_rows(u)] += fr[h, f_rows(u)].astype(F32)
 
     for i in range(CHUNKS):
         for dk in range(1, n_kv):
@@ -370,10 +400,10 @@
     each(1, per, lambda d: x_copy(d).wait_send())
     each(1, count, lambda d: dg_copy(d).wait_send())
     each(0, count, lambda d: dg_hop(d, dr_sem, core).wait_send())
-    for g in range(n_kv):
-        @pl.when(jnp.logical_or(grp != kv, kv != g))
-        def _():
-            f_copy(g).wait_send()
+    for dk in range(1, n_kv):
+        for u in range(PARTS):
+            f_cross(lax.rem(kv + dk, n_kv), u).wait_send()
+            f_along(fx, lax.rem(grp + dk, n_kv), u).wait_send()
 
 
 def local(n_seq, n_kv, plan, queries, keys, student_c, layer_input, b_weight):
@@ -412,10 +442,10 @@
             vmem((chips, rows, width), BF16), vmem((chips, rows, width), BF16),
             vmem((rows, width), F32),
             vmem((n_kv, per * rows, width), BF16),
-            vmem((n_kv, feat, width), BF16), vmem((n_kv, feat, width), BF16),
+            vmem((n_kv, feat, width), BF16), vmem((n_kv, feat, width), BF16), vmem((n_kv, feat, width), BF16),
             pair(chips), pair(chips), pair(n_kv * CHUNKS), pair(n_kv * CHUNKS), pair(n_kv),
             pair(per), pair(chips), pair(chips), pair(chips), pair(chips), pair(per // 2 * n_kv),
-            pair(per // 2 * n_kv), pair(n_kv), pltpu.SemaphoreType.DMA((3,)),
+            pair(per // 2 * n_kv), pair(n_kv * PARTS), pair(n_kv * PARTS), pltpu.SemaphoreType.DMA((3,)),
         ],
         compiler_params=pltpu.CompilerParams(
             collective_id=0, has_side_effects=True, vmem_limit_bytes=56 * 2**20

time: 66.9 us -> 62.7 us (0.937)
  Pallas kernels: 62.9 us -> 58.2 us
    pallas_call x1, Pallas kernels: 62.9 us -> 58.2 us  [local(): pl.pallas_call(functools.partial(kernel, n_seq, n_kv, rows, width, heads)...]
where the time goes in v3:
time: 62.7 us; the launch traced here: 62 us
  Pallas kernels  58.2 us (93%)
  local copies, waits for them, and re-layouts  3.24 us (5%)
  between operations  0.64 us (1%)
    pallas_call x1, Pallas kernels, local(): pl.pallas_call(functools.partial(kernel, n_seq, n_kv, rows, width, heads)...  58.2 us
    unnamed x2, local copies, waits for them, and re-layouts  3.24 us

profile of v3, /device:TPU:0, one launch (start us, length us, event | category | flops | bytes accessed | tf_op | source)
XLA Modules:
  0.0 62.0 jit_solution(3949188991583236881)
XLA Ops:
  0.6 58.2 %ssm_grad.1 = (bf16[128,512]{1,0:T(8,128)(2,1)}, f32[1,512,128]{2,1,0:T(8,128)}) custom-call(s32[16]{0:T(128)} %plan.1, bf16[128,512]{1,0:T(8,128)(2,1)} %q_ref.1, bf16[128,128]{1,0:T(8,128)(2,1)} %k_ref.1, bf16[128,512]{1,0:T(8,128)(2,1)} %c_ref.1, bf16[128,4096]{1,0:T(8,128)(2,1)} %x_any.1, bf16[1,8192,128]{2,1,0:T(8,128)(2,1)} %w_any.1), custom_call_target="tpu_custom_call" | custom-call | tf_op jit(solution)/shard_map/ssm_grad/pallas_call | solution.py:424
  58.8 1.6 %copy.10 = bf16[128,512]{1,0:T(8,128)(2,1)} copy(bf16[128,512]{1,0:T(8,128)(2,1)} %get-tuple-element.4) | data formatting | bytes 262144
  60.4 1.7 %copy.11 = f32[1,512,128]{2,1,0:T(8,128)} copy(f32[1,512,128]{2,1,0:T(8,128)} %get-tuple-element.5) | data formatting | bytes 524288
